TPU v7x, 256 devices: a whole 4x4x8 slice. The times are simulated.
256 devices in a mesh: wide: 32 (over x, y, core), narrow: 8 (over z).
Axes of the slice: x: 4, y: 4, z: 8, core: 2. Of those that a mesh axis runs over, the one named last changes fastest.
Arguments:
- tokens: bfloat16 [16384, 4096], P('wide', 'narrow'), may hold values from -40 to 40
- norm_gain: float32 [4096], P('narrow'), may hold values from 0.5 to 5
- w_query: bfloat16 [4096, 4096], P(None, 'narrow'), may hold values from -0.09375 to 0.09375
- key_weight: bfloat16 [4096, 1024], P(None, 'narrow'), may hold values from -0.09375 to 0.09375
- value_weight: bfloat16 [4096, 1024], P(None, 'narrow'), may hold values from -0.09375 to 0.09375
- w_out: bfloat16 [4096, 4096], P('narrow'), may hold values from -0.09375 to 0.09375
- doc_lengths: int32 [64], replicated, may hold values from 1 to 8192, 16384 in all
Outputs:
- attended: bfloat16 [16384, 4096], P('wide', 'narrow')
Inputs may be any that keep to these rules, and one draw needn't show every extreme that they name: `doc_lengths`: the lengths sum to 16384; the longest is exactly 8192.
All inputs are finite; a program needn't handle non-finite values.
Results may differ from a plain program's by a relative error of at most 0.019.
The roundings to bfloat16 on the way count: a program that leaves them out, or rounds other values in their place, can miss the bound.
Values may be sent and summed in bfloat16 or wider, within the bound.
No kernel may reach another device: no remote copies, remote signals or barrier semaphores. Data moves between devices by JAX's collectives and lax.ppermute only.
A program may use at most 128 MiB of HBM per device.

v0:
```python
import math
import jax
import jax.numpy as jnp
from jax import lax
from jax.sharding import PartitionSpec as P

MODEL_WIDTH = 4096
HEAD_SIZE = 128
EPSILON = 1e-05
ROPE_BASE = 500000.0
NEGATIVE = -1e30


def doc_of(lengths, positions):
    starts = jnp.cumsum(lengths) - lengths
    return jnp.sum((starts[None, :] <= positions[:, None]).astype(jnp.int32), axis=1) - 1


def doc_info(lengths, positions):
    starts = jnp.cumsum(lengths) - lengths
    docs = doc_of(lengths, positions)
    onehot = docs[:, None] == jnp.arange(lengths.shape[0], dtype=jnp.int32)[None, :]
    first_tok = jnp.sum(jnp.where(onehot, starts[None, :], 0), axis=1)
    return (docs, positions - first_tok)


def apply_rotary(values, rotary_positions):
    half_width = values.shape[-1] // 2
    frequency = ROPE_BASE ** (-(jnp.arange(half_width, dtype=jnp.float32) * 2.0 / values.shape[-1]))
    angles = rotary_positions.astype(jnp.float32)[:, None] * frequency[None, :]
    cosine = jnp.cos(angles)[:, None, :]
    sine_part = jnp.sin(angles)[:, None, :]
    first_half = values[..., :half_width]
    second_half = values[..., half_width:]
    return jnp.concatenate(
        [
            first_half * cosine - second_half * sine_part,
            second_half * cosine + first_half * sine_part,
        ],
        axis=-1,
    )


def per_device(tokens, norm_gain, w_query, key_weight, value_weight, w_out, doc_lengths):
    tok_rows = tokens.shape[0]
    wide_index = lax.axis_index("wide")
    as_float = tokens.astype(jnp.float32)
    squares = lax.psum(jnp.sum(as_float * as_float, axis=1), "narrow")
    inverse = lax.rsqrt(squares / MODEL_WIDTH + EPSILON)
    normed = (as_float * inverse[:, None] * norm_gain[None, :]).astype(jnp.bfloat16)
    shard_piece = lax.all_gather(normed, "narrow", axis=1, tiled=True)
    query_raw, key_unrotated, value_projected = tuple(
        (
            jnp.dot(shard_piece, matrix, preferred_element_type=jnp.float32)
            for matrix in (w_query, key_weight, value_weight)
        )
    )
    positions = wide_index * tok_rows + jnp.arange(tok_rows, dtype=jnp.int32)
    own_doc, rotary_positions = doc_info(doc_lengths, positions)
    heads_local = w_query.shape[1] // HEAD_SIZE
    kv_local = key_weight.shape[1] // HEAD_SIZE
    heads_per_group = heads_local // kv_local
    queries_own = (
        apply_rotary(query_raw.reshape(tok_rows, heads_local, HEAD_SIZE), rotary_positions)
        .astype(jnp.bfloat16)
        .reshape(tok_rows, kv_local, heads_per_group, HEAD_SIZE)
    )
    rotated_keys = apply_rotary(
        key_unrotated.reshape(tok_rows, kv_local, HEAD_SIZE), rotary_positions
    ).astype(jnp.bfloat16)
    values_cast = value_projected.reshape(tok_rows, kv_local, HEAD_SIZE).astype(jnp.bfloat16)
    key_value = jnp.stack([rotated_keys, values_cast])
    score_scale = 1.0 / math.sqrt(HEAD_SIZE)
    last_pos = jnp.max(positions)
    first_doc = jnp.min(own_doc)

    def update(carried, key_tile, value_tile, key_pos, key_doc):
        run_max, run_sum, accum = carried
        scores = (
            jnp.einsum("rkgd,nkd->kgrn", queries_own, key_tile, preferred_element_type=jnp.float32)
            * score_scale
        )
        allowed = (key_doc[None, :] == own_doc[:, None]) & (key_pos[None, :] <= positions[:, None])
        masked = jnp.where(allowed, scores, NEGATIVE)
        new_max = jnp.maximum(run_max, jnp.max(masked, axis=-1))
        weights = jnp.where(allowed, jnp.exp(scores - new_max[..., None]), 0.0)
        factor = jnp.exp(run_max - new_max)
        run_sum = run_sum * factor + jnp.sum(weights, axis=-1)
        accum = accum * factor[..., None] + jnp.einsum(
            "kgrn,nkd->kgrd",
            weights.astype(jnp.bfloat16),
            value_tile,
            preferred_element_type=jnp.float32,
        )
        return (new_max, run_sum, accum)

    start_status = (
        jnp.full((kv_local, heads_per_group, tok_rows), NEGATIVE, jnp.float32),
        jnp.zeros((kv_local, heads_per_group, tok_rows), jnp.float32),
        jnp.zeros((kv_local, heads_per_group, tok_rows, HEAD_SIZE), jnp.float32),
    )
    pair = lax.all_gather(key_value, "wide", axis=1, tiled=True)
    count_keys = pair.shape[1]
    tile_width = math.gcd(count_keys, 512)
    tile_count = count_keys // tile_width

    def tile_step(tile_index, carried_in):
        offset = tile_index * tile_width
        key_tile = lax.dynamic_slice_in_dim(pair, offset, tile_width, 1)
        key_pos = offset + jnp.arange(tile_width, dtype=jnp.int32)
        key_doc = doc_of(doc_lengths, key_pos)
        needed = (key_pos[0] <= last_pos) & (key_doc[-1] >= first_doc)
        return lax.cond(
            needed,
            lambda status: update(status, key_tile[0], key_tile[1], key_pos, key_doc),
            lambda status: status,
            carried_in,
        )

    status_now = lax.fori_loop(0, tile_count, tile_step, start_status)
    run_max, run_sum, accum = status_now
    heads_out = (
        (accum / run_sum[..., None])
        .transpose(2, 0, 1, 3)
        .reshape(tok_rows, heads_local * HEAD_SIZE)
        .astype(jnp.bfloat16)
    )
    partial_out = jnp.dot(heads_out, w_out, preferred_element_type=jnp.float32)
    return lax.psum_scatter(
        partial_out.astype(jnp.bfloat16), "narrow", scatter_dimension=1, tiled=True
    )


def solution(mesh):
    in_specs = (
        P("wide", "narrow"),
        P("narrow"),
        P(None, "narrow"),
        P(None, "narrow"),
        P(None, "narrow"),
        P("narrow", None),
        P(),
    )
    out_specs = P("wide", "narrow")
    return jax.shard_map(
        per_device, mesh=mesh, in_specs=in_specs, out_specs=out_specs, check_vma=False
    )
```

profile of v0, /device:TPU:1, one launch (start us, length us, event | category | flops | bytes accessed | tf_op | source)
XLA Modules:
  0.0 502.4 jit_solution(14981264105822187456)
XLA Ops:
  6.5 1.3 fusion.25
  7.8 17.3 %psum.7 = f32[512]{0:T(512)S(1)} all-reduce(f32[512]{0:T(512)S(1)} %fusion.25), channel_id=1, replica_groups=mesh['wide'=32,'narrow'=8] {'narrow'}, use_global_device_ids=true, to_apply=%region_1.0 | all-reduce | flops 512 | bytes 4096 | tf_op jit(solution)/shard_map/psum | solution.py:48
  25.2 2.0 fusion.27
  29.9 54.0 %all-gather.3.cloned.1.call-done = bf16[512,4096]{1,0:T(8,128)(2,1)} async-done(((bf16[512,512]{1,0:T(8,128)(2,1)}), bf16[512,4096]{1,0:T(8,128)(2,1)}) %all-gather.3.cloned.1.call-update) | async-done | bytes 4194320 | tf_op jit(solution)/shard_map/all_gather | solution.py:51
  83.9 3.8 convolution_bitcast_fusion
  88.3 1.5 fusion.24
  91.5 1.7 multiply_cosine_fusion
  93.2 5.8 %fusion.43 = f32[512,512]{0,1:T(8,128)S(1)} fusion(bf16[512,4096]{1,0:T(8,128)(2,1)} %all-gather.3.cloned.1.call-done, bf16[4096,512]{1,0:T(8,128)(2,1)} %param.13), kind=kOutput, calls=%fused_computation.71 | convolution fusion | flops 2147483648 | bytes 9437184 | tf_op jit(solution)/shard_map/dot_general | solution.py:54
  100.3 1.4 copy.31
  101.7 1.2 fusion.28
  103.2 51.1 %all-gather.5.cloned.1.call-done = bf16[2,16384,1,128]{1,3,2,0:T(8,128)(2,1)} async-done(((bf16[2,512,1,128]{1,3,2,0:T(8,128)(2,1)}), bf16[2,16384,1,128]{1,3,2,0:T(8,128)(2,1)}) %all-gather.5.cloned.1.call-update) | async-done | bytes 8388624 | tf_op jit(solution)/shard_map/all_gather | solution.py:102
  154.3 11.9 %copy.26 = bf16[2,16384,1,128]{3,1,2,0:T(8,128)(2,1)} copy(bf16[2,16384,1,128]{1,3,2,0:T(8,128)(2,1)} %all-gather.5.cloned.1.call-done) | data formatting | bytes 16777216
  166.3 134.6 %while.20 = (s32[]{:T(128)}, f32[1,4,512]{2,1,0:T(4,128)S(1)}, f32[1,4,512]{2,1,0:T(4,128)S(1)}, f32[1,4,512,128]{3,2,1,0:T(8,128)S(1)}, s32[]{:T(128)}, /*index...) while((s32[]{:T(128)}, f32[1,4,512]{2,1,0:T(4,128)S(1)}, ...), condition=%wide.region_13.14_spmd.clone, body=%wide.region_7.13_spmd.clone.sunk | while | flops 549821440 | bytes 33448608 | solution.py:120
  169.9 8.8 %conditional.3 = ((f32[1,4,512]{2,1,0:T(4,128)S(1)}, f32[1,4,512]{2,1,0:T(4,128)S(1)}, f32[1,4,512,128]{3,2,1,0:T(8,128)S(1)})) conditional(s32[]{:T(128)} %convert_element_type.114, (f32[1,4,512]{2,1,0:T(4,128)S(1)}, f32[1,4,512]{2,1,0:T(4,128)S(1)}, f32[1,4,512,128]{3,2,1,0:T(8,128)S(1)}) %tuple.65, (s32[512]{0:T(512)S(1)}, s32[512]{0:T(512)S(1)}, ...), branch_computations={%region_9.9_spmd, %region_10.12_spmd} | conditional | flops 549722624 | bytes 33435770 | solution.py:113
  170.2 3.7 fusion.2
  174.0 3.8 fusion.14
  177.8 0.9 fusion.6
  182.4 8.8 %conditional.3 = ((f32[1,4,512]{2,1,0:T(4,128)S(1)}, f32[1,4,512]{2,1,0:T(4,128)S(1)}, f32[1,4,512,128]{3,2,1,0:T(8,128)S(1)})) conditional(s32[]{:T(128)} %convert_element_type.114, (f32[1,4,512]{2,1,0:T(4,128)S(1)}, f32[1,4,512]{2,1,0:T(4,128)S(1)}, f32[1,4,512,128]{3,2,1,0:T(8,128)S(1)}) %tuple.65, (s32[512]{0:T(512)S(1)}, s32[512]{0:T(512)S(1)}, ...), branch_computations={%region_9.9_spmd, %region_10.12_spmd} | conditional | flops 549722624 | bytes 33435770 | solution.py:113
  182.7 3.7 fusion.2
  186.5 3.8 fusion.14
  300.9 1.3 copy.27
  302.2 1.4 divide_convert_fusion
  303.6 6.5 %convolution_convert_fusion = bf16[512,4096]{1,0:T(8,128)(2,1)} fusion(bf16[512,512]{0,1:T(8,128)(2,1)S(1)} %bitcast.96, bf16[512,4096]{1,0:T(8,128)(2,1)} %param.16), kind=kOutput, calls=%fused_computation.30 | convolution fusion | flops 2149580800 | bytes 8912896 | tf_op jit(solution)/shard_map/dot_general | solution.py:128
  310.1 185.8 %reduce-scatter.2.cloned.1.call-done = bf16[512,512]{1,0:T(8,128)(2,1)} async-done(((bf16[512,4096]{1,0:T(8,128)(2,1)}), bf16[512,512]{1,0:T(8,128)(2,1)}) %reduce-scatter.2.cloned.1.call-update) | async-done | bytes 524304 | tf_op jit(solution)/shard_map/reduce_scatter | solution.py:129
  (269 shorter events, 45.1 us)
Async XLA Ops:
  6.5 77.4 %copy-start = (bf16[4096,128]{1,0:T(8,128)(2,1)S(1)}, bf16[4096,128]{1,0:T(8,128)(2,1)}, u32[]{:S(2)}) copy-start(bf16[4096,128]{1,0:T(8,128)(2,1)} %param.14) | copy-start | bytes 3145732
  6.5 77.4 %all-gather.3.cloned.1.call-start = ((), (), s32[]{:S(2)}) async-start(), calls=%async_computation.1 | async-start | bytes 4718592 | tf_op jit(solution)/shard_map/all_gather | solution.py:51
  27.2 61.1 %copy-start.3 = (bf16[4096,128]{1,0:T(8,128)(2,1)S(1)}, bf16[4096,128]{1,0:T(8,128)(2,1)}, u32[]{:S(2)}) copy-start(bf16[4096,128]{1,0:T(8,128)(2,1)} %param.15) | copy-start | bytes 3145732
  27.2 127.1 %all-gather.5.cloned.1.call-start = ((), (), s32[]{:S(2)}) async-start(), calls=%async_computation.2 | async-start | bytes 8650752 | tf_op jit(solution)/shard_map/all_gather | solution.py:102
  83.9 4.4 copy-start.2
  90.6 405.3 %reduce-scatter.2.cloned.1.call-start = ((), (), s32[]{:S(2)}) async-start(), calls=%async_computation.3 | async-start | bytes 4718592 | tf_op jit(solution)/shard_map/reduce_scatter | solution.py:129
  174.0 3.8 copy-start.1
  186.5 3.8 copy-start.1
Sparse Core Ops, SparseCore 0:
  27.3 56.5 all-gather.2
  90.7 63.5 all-gather.4
  310.2 185.6 reduce-scatter.1
where the time goes:
time: 505 us; the launch traced here: 502 us
  waiting for transfers between devices  291 us (58%)
  loops' own time  80.4 us (16%)
  local copies, waits for them, and re-layouts  50.1 us (10%)
  matrix products  32.8 us (6%)
  other arithmetic  17.4 us (3%)
  blocking collectives  17.3 us (3%)
  between operations  13.2 us (3%)
    reduce_scatter x1, waiting for transfers between devices, per_device(): lax.psum_scatter(partial_out.astype(jnp.bfloat16), 'narrow', scatter_dime...  186 us
    another operation x1, loops' own time, per_device(): status_now = lax.fori_loop(0, tile_count, tile_step, start_status)  79.9 us
    all_gather x1, waiting for transfers between devices, per_device(): shard_piece = lax.all_gather(normed, 'narrow', axis=1, tiled=True)  54 us
    all_gather x1, waiting for transfers between devices, per_device(): pair = lax.all_gather(key_value, 'wide', axis=1, tiled=True)  51.1 us
    slice x64, local copies, waits for them, and re-layouts, tile_step(): needed = (key_pos[0] <= last_pos) & (key_doc[-1] >= first_doc)  33.3 us
    psum x1, blocking collectives, per_device(): squares = lax.psum(jnp.sum(as_float * as_float, axis=1), 'narrow')  17.3 us
    unnamed x9, local copies, waits for them, and re-layouts  13.6 us
    dot_general x3, matrix products, per_device(): jnp.dot(shard_piece, matrix, preferred_element_type=jnp.float32)  11.2 us
  transfers between devices with their start and end apart: 3, of which 3 were waited for; matrix products, arithmetic and copies ran while one was open for 3% of the time, Pallas kernels for 0%

commit v1 on v0

--- a/solution.py
+++ b/solution.py
@@ -48,7 +48,14 @@
     squares = lax.psum(jnp.sum(as_float * as_float, axis=1), "narrow")
     inverse = lax.rsqrt(squares / MODEL_WIDTH + EPSILON)
     normed = (as_float * inverse[:, None] * norm_gain[None, :]).astype(jnp.bfloat16)
-    shard_piece = lax.all_gather(normed, "narrow", axis=1, tiled=True)
+    ring = [normed]
+    for hop in range(7):
+        ring.append(lax.ppermute(ring[-1], "narrow", [(dev, (dev + 1) % 8) for dev in range(8)]))
+    shard_piece = jnp.roll(
+        jnp.concatenate(ring[::-1], axis=1),
+        (lax.axis_index("narrow") + 1) * ring[0].shape[1],
+        axis=1,
+    )
     query_raw, key_unrotated, value_projected = tuple(
         (
             jnp.dot(shard_piece, matrix, preferred_element_type=jnp.float32)

time: 505 us -> 555 us (1.099)
  waiting for transfers between devices: 291 us -> 331 us
  local copies, waits for them, and re-layouts: 50.1 us -> 57 us
    ppermute x0 -> x7, waiting for transfers between devices: none -> 83 us  [per_device(): lax.ppermute(ring[-1], 'narrow', [(dev, (dev + 1) % 8) for dev in range(8)])]
    all_gather x1 -> x0, waiting for transfers between devices: 54 us -> none  [per_device(): shard_piece = lax.all_gather(normed, 'narrow', axis=1, tiled=True)]
    all_gather x1, waiting for transfers between devices: 51.1 us -> 62.3 us  [per_device(): pair = lax.all_gather(key_value, 'wide', axis=1, tiled=True)]
    unnamed x9 -> x31, local copies, waits for them, and re-layouts: 13.6 us -> 20.6 us
  transfers between devices with their start and end apart: 3 -> 9, of which waited for: 3 -> 9; matrix products, arithmetic and copies ran while one was open for 3% -> 3% of each run, Pallas kernels for 0% -> 0%
where the time goes in v1:
time: 555 us; the launch traced here: 550 us
  waiting for transfers between devices  331 us (60%)
  loops' own time  83.1 us (15%)
  local copies, waits for them, and re-layouts  57 us (10%)
  matrix products  30.5 us (5%)
  blocking collectives  17.3 us (3%)
  other arithmetic  17.1 us (3%)
  between operations  13.7 us (2%)
    reduce_scatter x1, waiting for transfers between devices, per_device(): lax.psum_scatter(partial_out.astype(jnp.bfloat16), 'narrow', scatter_dime...  186 us
    ppermute x7, waiting for transfers between devices, per_device(): lax.ppermute(ring[-1], 'narrow', [(dev, (dev + 1) % 8) for dev in range(8)])  83 us
    another operation x1, loops' own time, per_device(): status_now = lax.fori_loop(0, tile_count, tile_step, start_status)  82.6 us
    all_gather x1, waiting for transfers between devices, per_device(): pair = lax.all_gather(key_value, 'wide', axis=1, tiled=True)  62.3 us
    slice x64, local copies, waits for them, and re-layouts, tile_step(): needed = (key_pos[0] <= last_pos) & (key_doc[-1] >= first_doc)  33.3 us
    unnamed x31, local copies, waits for them, and re-layouts  20.6 us
    psum x1, blocking collectives, per_device(): squares = lax.psum(jnp.sum(as_float * as_float, axis=1), 'narrow')  17.3 us
  transfers between devices with their start and end apart: 9, of which 9 were waited for; matrix products, arithmetic and copies ran while one was open for 3% of the time, Pallas kernels for 0%

profile of v1, /device:TPU:1, one launch (start us, length us, event | category | flops | bytes accessed | tf_op | source)
XLA Modules:
  0.0 550.1 jit_solution(17790930764973695096)
XLA Ops:
  7.9 17.3 %psum.7 = f32[512]{0:T(512)S(1)} all-reduce(f32[512]{0:T(512)S(1)} %fusion.39), channel_id=1, replica_groups=mesh['wide'=32,'narrow'=8] {'narrow'}, use_global_device_ids=true, to_apply=%region_1.0 | all-reduce | flops 512 | bytes 4096 | tf_op jit(solution)/shard_map/psum | solution.py:48
  26.5 10.4 %collective-permute-done = bf16[512,512]{1,0:T(8,128)(2,1)S(1)} collective-permute-done((bf16[512,512]{1,0:T(8,128)(2,1)S(1)}, bf16[512,512]{1,0:T(8,128)(2,1)S(1)}, u32[]{:S(2)}, u32[]{:S(2)}) %collective-permute-start) | collective-permute-done | bytes 524320 | tf_op jit(solution)/shard_map/ppermute | solution.py:53
  36.9 10.4 %collective-permute-done.1 = bf16[512,512]{1,0:T(8,128)(2,1)S(1)} collective-permute-done((bf16[512,512]{1,0:T(8,128)(2,1)S(1)}, bf16[512,512]{1,0:T(8,128)(2,1)S(1)}, u32[]{:S(2)}, u32[]{:S(2)}) %collective-permute-start.1) | collective-permute-done | bytes 524320 | tf_op jit(solution)/shard_map/ppermute | solution.py:53
  47.3 10.9 %collective-permute-done.2 = bf16[512,512]{1,0:T(8,128)(2,1)S(1)} collective-permute-done((bf16[512,512]{1,0:T(8,128)(2,1)S(1)}, bf16[512,512]{1,0:T(8,128)(2,1)S(1)}, u32[]{:S(2)}, u32[]{:S(2)}) %collective-permute-start.2) | collective-permute-done | bytes 524320 | tf_op jit(solution)/shard_map/ppermute | solution.py:53
  58.2 12.0 %collective-permute-done.3 = bf16[512,512]{1,0:T(8,128)(2,1)S(1)} collective-permute-done((bf16[512,512]{1,0:T(8,128)(2,1)S(1)}, bf16[512,512]{1,0:T(8,128)(2,1)S(1)}, u32[]{:S(2)}, u32[]{:S(2)}) %collective-permute-start.3) | collective-permute-done | bytes 524320 | tf_op jit(solution)/shard_map/ppermute | solution.py:53
  71.0 12.4 %collective-permute-done.4 = bf16[512,512]{1,0:T(8,128)(2,1)} collective-permute-done((bf16[512,512]{1,0:T(8,128)(2,1)S(1)}, bf16[512,512]{1,0:T(8,128)(2,1)}, u32[]{:S(2)}, u32[]{:S(2)}) %collective-permute-start.4) | collective-permute-done | bytes 524320 | tf_op jit(solution)/shard_map/ppermute | solution.py:53
  85.1 12.4 %collective-permute-done.5 = bf16[512,512]{1,0:T(8,128)(2,1)} collective-permute-done((bf16[512,512]{1,0:T(8,128)(2,1)}, bf16[512,512]{1,0:T(8,128)(2,1)}, u32[]{:S(2)}, u32[]{:S(2)}) %collective-permute-start.5) | collective-permute-done | bytes 524320 | tf_op jit(solution)/shard_map/ppermute | solution.py:53
  98.4 14.5 %collective-permute-done.6 = bf16[512,512]{1,0:T(8,128)(2,1)S(1)} collective-permute-done((bf16[512,512]{1,0:T(8,128)(2,1)}, bf16[512,512]{1,0:T(8,128)(2,1)S(1)}, u32[]{:S(2)}, u32[]{:S(2)}) %collective-permute-start.6) | collective-permute-done | bytes 524320 | tf_op jit(solution)/shard_map/ppermute | solution.py:53
  119.6 1.5 fusion.30
  121.2 1.5 fusion.36
  125.0 1.7 multiply_cosine_fusion
  126.7 5.8 %fusion.24 = f32[512,512]{0,1:T(8,128)S(1)} fusion(bf16[4096,512]{1,0:T(8,128)(2,1)} %param.13, bf16[512,8192]{1,0:T(8,128)(2,1)} %copy-done.5, s32[]{:T(128)S(6)} %select_n.37), kind=kOutput, calls=%fused_computation.31 | convolution fusion | flops 2147483648 | bytes 9437188 | tf_op jit(solution)/shard_map/dot_general | solution.py:61
  133.8 1.4 copy.31
  136.7 62.3 %all-gather.2.cloned.1.call-done = bf16[2,16384,1,128]{1,3,2,0:T(8,128)(2,1)} async-done(((bf16[2,512,1,128]{1,3,2,0:T(8,128)(2,1)}), bf16[2,16384,1,128]{1,3,2,0:T(8,128)(2,1)}) %all-gather.2.cloned.1.call-update) | async-done | bytes 8388624 | tf_op jit(solution)/shard_map/all_gather | solution.py:109
  199.0 11.9 %copy.26 = bf16[2,16384,1,128]{3,1,2,0:T(8,128)(2,1)} copy(bf16[2,16384,1,128]{1,3,2,0:T(8,128)(2,1)} %all-gather.2.cloned.1.call-done) | data formatting | bytes 16777216
  211.0 137.3 %while.20 = (s32[]{:T(128)}, f32[1,4,512]{2,1,0:T(4,128)S(1)}, f32[1,4,512]{2,1,0:T(4,128)S(1)}, f32[1,4,512,128]{3,2,1,0:T(8,128)S(1)}, s32[]{:T(128)}, /*index...) while((s32[]{:T(128)}, f32[1,4,512]{2,1,0:T(4,128)S(1)}, ...), condition=%wide.region_13.14_spmd.clone, body=%wide.region_7.13_spmd.clone.sunk | while | flops 549821440 | bytes 33448608 | solution.py:127
  214.7 8.9 %conditional.3 = ((f32[1,4,512]{2,1,0:T(4,128)S(1)}, f32[1,4,512]{2,1,0:T(4,128)S(1)}, f32[1,4,512,128]{3,2,1,0:T(8,128)S(1)})) conditional(s32[]{:T(128)} %convert_element_type.122, (f32[1,4,512]{2,1,0:T(4,128)S(1)}, f32[1,4,512]{2,1,0:T(4,128)S(1)}, f32[1,4,512,128]{3,2,1,0:T(8,128)S(1)}) %tuple.65, (s32[512]{0:T(512)S(1)}, s32[512]{0:T(512)S(1)}, ...), branch_computations={%region_9.9_spmd, %region_10.12_spmd} | conditional | flops 549722624 | bytes 33435770 | solution.py:120
  215.0 3.7 fusion.2
  218.8 3.8 fusion.14
  227.3 8.8 %conditional.3 = ((f32[1,4,512]{2,1,0:T(4,128)S(1)}, f32[1,4,512]{2,1,0:T(4,128)S(1)}, f32[1,4,512,128]{3,2,1,0:T(8,128)S(1)})) conditional(s32[]{:T(128)} %convert_element_type.122, (f32[1,4,512]{2,1,0:T(4,128)S(1)}, f32[1,4,512]{2,1,0:T(4,128)S(1)}, f32[1,4,512,128]{3,2,1,0:T(8,128)S(1)}) %tuple.65, (s32[512]{0:T(512)S(1)}, s32[512]{0:T(512)S(1)}, ...), branch_computations={%region_9.9_spmd, %region_10.12_spmd} | conditional | flops 549722624 | bytes 33435770 | solution.py:120
  227.6 3.7 fusion.2
  231.4 3.8 fusion.14
  351.0 6.5 %convolution_convert_fusion = bf16[512,4096]{1,0:T(8,128)(2,1)} fusion(bf16[512,512]{0,1:T(8,128)(2,1)S(1)} %bitcast.93, bf16[512,4096]{1,0:T(8,128)(2,1)} %param.16), kind=kOutput, calls=%fused_computation.30 | convolution fusion | flops 2149580800 | bytes 8912896 | tf_op jit(solution)/shard_map/dot_general | solution.py:135
  357.5 185.8 %reduce-scatter.2.cloned.1.call-done = bf16[512,512]{1,0:T(8,128)(2,1)} async-done(((bf16[512,4096]{1,0:T(8,128)(2,1)}), bf16[512,512]{1,0:T(8,128)(2,1)}) %reduce-scatter.2.cloned.1.call-update) | async-done | bytes 524304 | tf_op jit(solution)/shard_map/reduce_scatter | solution.py:136
  (304 shorter events, 59.8 us)
Async XLA Ops:
  6.5 113.1 %copy-start = (bf16[4096,128]{1,0:T(8,128)(2,1)S(1)}, bf16[4096,128]{1,0:T(8,128)(2,1)}, u32[]{:S(2)}) copy-start(bf16[4096,128]{1,0:T(8,128)(2,1)} %param.14) | copy-start | bytes 3145732
  6.5 110.0 %copy-start.2 = (bf16[512,512]{1,0:T(8,128)(2,1)S(1)}, bf16[512,512]{1,0:T(8,128)(2,1)}, u32[]{:S(2)}) copy-start(bf16[512,512]{1,0:T(8,128)(2,1)} %param.11) | copy-start | bytes 1572868
  6.5 110.0 %copy-start.6 = (f32[512]{0:T(512)S(1)}, f32[512]{0:T(512)}, u32[]{:S(2)}) copy-start(f32[512]{0:T(512)} %param.12) | copy-start | bytes 6148
  6.5 192.4 %all-gather.2.cloned.1.call-start = ((), (), s32[]{:S(2)}) async-start(), calls=%async_computation.1 | async-start | bytes 8650752 | tf_op jit(solution)/shard_map/all_gather | solution.py:109
  26.4 10.5 %collective-permute-start = (bf16[512,512]{1,0:T(8,128)(2,1)S(1)}, bf16[512,512]{1,0:T(8,128)(2,1)S(1)}, u32[]{:S(2)}, u32[]{:S(2)}) collective-permute-start(bf16[512,512]{1,0:T(8,128)(2,1)S(1)} %fusion.41), channel_id=1, source_target_pairs={{0,1},{1,2},{2,3},{3,4},{4,5},{5,6},{6,7},{7,0},{8,9},{9,10},{10,1... | collective-permute-start | bytes 1572872 | tf_op jit(solution)/shard_map/ppermute | solution.py:53
  36.9 10.4 %collective-permute-start.1 = (bf16[512,512]{1,0:T(8,128)(2,1)S(1)}, bf16[512,512]{1,0:T(8,128)(2,1)S(1)}, u32[]{:S(2)}, u32[]{:S(2)}) collective-permute-start(bf16[512,512]{1,0:T(8,128)(2,1)S(1)} %collective-permute-done), channel_id=1, source_target_pairs={{0,1},{1,2},{2,3},{3,4},{4,5},{5,6},{6,7},{7,0},{8,9},{9,10},{10,1... | collective-permute-start | bytes 1572872 | tf_op jit(solution)/shard_map/ppermute | solution.py:53
  47.3 10.9 %collective-permute-start.2 = (bf16[512,512]{1,0:T(8,128)(2,1)S(1)}, bf16[512,512]{1,0:T(8,128)(2,1)S(1)}, u32[]{:S(2)}, u32[]{:S(2)}) collective-permute-start(bf16[512,512]{1,0:T(8,128)(2,1)S(1)} %collective-permute-done.1), channel_id=1, source_target_pairs={{0,1},{1,2},{2,3},{3,4},{4,5},{5,6},{6,7},{7,0},{8,9},{9,10},{10,1... | collective-permute-start | bytes 1572872 | tf_op jit(solution)/shard_map/ppermute | solution.py:53
  58.2 12.0 %collective-permute-start.3 = (bf16[512,512]{1,0:T(8,128)(2,1)S(1)}, bf16[512,512]{1,0:T(8,128)(2,1)S(1)}, u32[]{:S(2)}, u32[]{:S(2)}) collective-permute-start(bf16[512,512]{1,0:T(8,128)(2,1)S(1)} %collective-permute-done.2), channel_id=1, source_target_pairs={{0,1},{1,2},{2,3},{3,4},{4,5},{5,6},{6,7},{7,0},{8,9},{9,10},{10,1... | collective-permute-start | bytes 1572872 | tf_op jit(solution)/shard_map/ppermute | solution.py:53
  70.2 0.8 copy-start.3
  71.0 12.4 %collective-permute-start.4 = (bf16[512,512]{1,0:T(8,128)(2,1)S(1)}, bf16[512,512]{1,0:T(8,128)(2,1)}, u32[]{:S(2)}, u32[]{:S(2)}) collective-permute-start(bf16[512,512]{1,0:T(8,128)(2,1)S(1)} %collective-permute-done.3), channel_id=1, source_target_pairs={{0,1},{1,2},{2,3},{3,4},{4,5},{5,6},{6,7},{7,0},{8,9},{9,10},{10,1... | collective-permute-start | bytes 1572872 | tf_op jit(solution)/shard_map/ppermute | solution.py:53
  83.4 14.2 %collective-permute-start.5 = (bf16[512,512]{1,0:T(8,128)(2,1)}, bf16[512,512]{1,0:T(8,128)(2,1)}, u32[]{:S(2)}, u32[]{:S(2)}) collective-permute-start(bf16[512,512]{1,0:T(8,128)(2,1)} %collective-permute-done.4), channel_id=1, source_target_pairs={{0,1},{1,2},{2,3},{3,4},{4,5},{5,6},{6,7},{7,0},{8,9},{9,10},{10,1... | collective-permute-start | bytes 1572872 | tf_op jit(solution)/shard_map/ppermute | solution.py:53
  85.0 34.1 %copy-start.4 = (bf16[512,512]{1,0:T(8,128)(2,1)S(1)}, bf16[512,512]{1,0:T(8,128)(2,1)}, u32[]{:S(2)}) copy-start(bf16[512,512]{1,0:T(8,128)(2,1)} %copy-done.3) | copy-start | bytes 1572868
  97.6 15.3 %collective-permute-start.6 = (bf16[512,512]{1,0:T(8,128)(2,1)}, bf16[512,512]{1,0:T(8,128)(2,1)S(1)}, u32[]{:S(2)}, u32[]{:S(2)}) collective-permute-start(bf16[512,512]{1,0:T(8,128)(2,1)} %collective-permute-done.5), channel_id=1, source_target_pairs={{0,1},{1,2},{2,3},{3,4},{4,5},{5,6},{6,7},{7,0},{8,9},{9,10},{10,1... | collective-permute-start | bytes 1572872 | tf_op jit(solution)/shard_map/ppermute | solution.py:53
  116.5 4.7 copy-start.7
  119.6 3.7 copy-start.5
  124.0 419.3 %reduce-scatter.2.cloned.1.call-start = ((), (), s32[]{:S(2)}) async-start(), calls=%async_computation.2 | async-start | bytes 4718592 | tf_op jit(solution)/shard_map/reduce_scatter | solution.py:136
  218.8 3.8 copy-start.1
  231.4 3.8 copy-start.1
Sparse Core Ops, SparseCore 0:
  124.2 74.7 all-gather.1
  357.6 185.6 reduce-scatter.1
